TPU v7x, 256 devices: a whole 4x4x8 slice. The times are simulated.
256 devices in a mesh: seq: 32 (over y, x, core), head: 8 (over z).
Axes of the slice: x: 4, y: 4, z: 8, core: 2. Of those that a mesh axis runs over, the one named last changes fastest.
Arguments:
- queries: bfloat16 [32768, 4096], P('seq', 'head'), may hold values from -6 to 6
- keys: bfloat16 [32768, 4096], P('seq', 'head'), may hold values from -6 to 6
- values: bfloat16 [32768, 4096], P('seq', 'head'), may hold values from -6 to 6
- out_grad: bfloat16 [32768, 4096], P('seq', 'head'), may hold values from -6 to 6
- out_weight: bfloat16 [4096, 4096], P('head'), may hold values from -0.125 to 0.125
Outputs:
- query_gradient: bfloat16 [32768, 4096], P('seq', 'head')
- key_grad: bfloat16 [32768, 4096], P('seq', 'head')
- value_grad: bfloat16 [32768, 4096], P('seq', 'head')
All inputs are finite; a program needn't handle non-finite values.
Results may differ from a plain program's by a relative error of at most 0.014.
Values may be sent and summed in bfloat16 or wider, within the bound.
A program may use at most 192 MiB of HBM per device.

v0:
```python
import math

import jax
import jax.numpy as jnp
from jax import lax
from jax.sharding import PartitionSpec as P

HD = 128


def on_device(queries, keys, values, out_grad, out_weight):
    tok_rows = queries.shape[0]
    local_width = out_weight.shape[0]
    heads_here = local_width // HD
    factor = 1.0 / math.sqrt(HD * tok_rows * lax.axis_size("seq"))
    head_grad = lax.dot_general(
        lax.all_gather(out_grad, "head", axis=1, tiled=True),
        out_weight,
        (((1,), (1,)), ((), ())),
        preferred_element_type=jnp.float32,
    ).astype(jnp.bfloat16)
    query_h = queries.reshape(tok_rows, heads_here, HD)
    key_heads = keys.reshape(tok_rows, heads_here, HD)
    value_heads = values.reshape(tok_rows, heads_here, HD)
    gradient_heads = head_grad.reshape(tok_rows, heads_here, HD)
    key_running_state = jnp.einsum(
        "buq,bud->uqd", key_heads, value_heads, preferred_element_type=jnp.float32
    )
    query_state = jnp.einsum(
        "thq,tho->hqo", query_h, gradient_heads, preferred_element_type=jnp.float32
    )
    position = lax.axis_index("seq")
    portions = (
        lax.all_gather(
            key_running_state[None].astype(jnp.bfloat16), "seq", axis=0, tiled=True
        ).astype(jnp.float32),
        lax.all_gather(query_state[None].astype(jnp.bfloat16), "seq", axis=0, tiled=True).astype(
            jnp.float32
        ),
    )
    shard_ids = jnp.arange(portions[0].shape[0], dtype=jnp.int32)
    keep_early = (shard_ids < position)[:, None, None, None]
    keep_late = (shard_ids > position)[:, None, None, None]
    prefix_total = jnp.zeros_like(key_running_state) + jnp.sum(
        jnp.where(keep_early, portions[0], 0.0), axis=0
    )
    suffix = jnp.zeros_like(query_state) + jnp.sum(jnp.where(keep_late, portions[1], 0.0), axis=0)
    prefix_total = prefix_total.astype(jnp.bfloat16)
    suffix = suffix.astype(jnp.bfloat16)
    causal = (jnp.arange(tok_rows)[:, None] >= jnp.arange(tok_rows)[None, :])[None]
    score_gradient = jnp.where(
        causal,
        jnp.einsum("tho,sho->hts", gradient_heads, value_heads, preferred_element_type=jnp.float32),
        0.0,
    ).astype(jnp.bfloat16)
    attn_scores = jnp.where(
        causal,
        jnp.einsum("thk,shk->hts", query_h, key_heads, preferred_element_type=jnp.float32),
        0.0,
    ).astype(jnp.bfloat16)
    query_gradient = jnp.einsum(
        "ryx,xrj->yrj", score_gradient, key_heads, preferred_element_type=jnp.float32
    ) + jnp.einsum("lmp,mgp->lmg", gradient_heads, prefix_total, preferred_element_type=jnp.float32)
    key_grad = jnp.einsum(
        "hts,thq->shq", score_gradient, query_h, preferred_element_type=jnp.float32
    ) + jnp.einsum("sho,hqo->shq", value_heads, suffix, preferred_element_type=jnp.float32)
    value_grad = jnp.einsum(
        "hts,tho->sho", attn_scores, gradient_heads, preferred_element_type=jnp.float32
    ) + jnp.einsum("shq,hqo->sho", key_heads, suffix, preferred_element_type=jnp.float32)
    return (
        (factor * query_gradient).astype(jnp.bfloat16).reshape(tok_rows, local_width),
        (factor * key_grad).astype(jnp.bfloat16).reshape(tok_rows, local_width),
        (factor * value_grad).astype(jnp.bfloat16).reshape(tok_rows, local_width),
    )


def solution(mesh):
    placed = (
        P("seq", "head"),
        P("seq", "head"),
        P("seq", "head"),
        P("seq", "head"),
        P("head", None),
    )
    return jax.shard_map(
        on_device,
        mesh=mesh,
        in_specs=placed,
        out_specs=(P("seq", "head"), P("seq", "head"), P("seq", "head")),
        check_vma=False,
    )
```

profile of v0, /device:TPU:1, one launch (start us, length us, event | category | flops | bytes accessed | tf_op | source)
XLA Modules:
  0.0 236.8 jit_solution(7215017661648151623)
XLA Ops:
  7.2 0.0 copy-start
  7.2 0.0 all-gather.6.cloned.1.call-start
  7.2 0.7 all-gather.6.cloned.1.call-update
  7.9 0.0 all-gather.8.cloned.1.call-start
  8.0 0.4 copy-done
  8.4 2.4 convolution_convert_fusion.2
  10.8 0.0 all-gather.8.cloned.1.call-update
  10.8 0.0 copy-start.5
  10.8 0.0 all-gather.10.cloned.1.call-start
  10.8 96.9 %all-gather.6.cloned.1.call-done = bf16[1024,4096]{1,0:T(8,128)(2,1)} async-done(((bf16[1024,512]{1,0:T(8,128)(2,1)}), bf16[1024,4096]{1,0:T(8,128)(2,1)}) %all-gather.6.cloned.1.call-update) | async-done | bytes 8388624 | tf_op jit(solution)/shard_map/all_gather | solution.py:17
  107.8 9.1 %convolution_convert_fusion = bf16[1024,512]{0,1:T(8,128)(2,1)S(1)} fusion(bf16[1024,4096]{1,0:T(8,128)(2,1)} %all-gather.6.cloned.1.call-done, bf16[512,4096]{1,0:T(8,128)(2,1)} %param.9), kind=kOutput, calls=%fused_computation.15 | convolution fusion | flops 4295491584 | bytes 13631488 | tf_op jit(solution)/shard_map/dot_general | solution.py:16
  116.8 0.0 copy-start.7
  116.9 1.0 copy-done.7
  117.8 0.0 copy-done.5
  117.8 0.5 fusion.7
  118.3 0.8 copy.31
  119.1 0.0 all-gather.10.cloned.1.call-update
  119.1 0.3 iota_compare_fusion
  119.4 0.0 copy-start.6
  119.4 41.6 %all-gather.8.cloned.1.call-done = bf16[128,128,128]{2,1,0:T(8,128)(2,1)} async-done(((bf16[4,128,128]{2,1,0:T(8,128)(2,1)}), bf16[128,128,128]{2,1,0:T(8,128)(2,1)}) %all-gather.8.cloned.1.call-update) | async-done | bytes 4194320 | tf_op jit(solution)/shard_map/all_gather | solution.py:34
  161.1 0.0 copy-start.8
  161.1 3.3 %fusion.1 = bf16[4,128,128]{2,1,0:T(8,128)(2,1)S(1)} fusion(bf16[32,4,128,128]{3,2,1,0:T(8,128)(2,1)} %bitcast.100, pred[32]{0:T(512)(128)(4,1)S(1)} %iota_compare_fusion.2), kind=kLoop, calls=%fused_computation.5 | loop fusion | flops 6225920 | bytes 4325408 | tf_op jit(solution)/shard_map/reduce_sum | solution.py:44
  164.4 0.0 copy-done.8
  164.4 0.0 copy-start.2
  164.4 2.7 %select_convert_fusion.1 = bf16[4,1024,1024]{2,1,0:T(8,128)(2,1)S(1)} fusion(bf16[1024,4,128]{0,2,1:T(8,128)(2,1)S(1)} %bitcast.106, pred[1024,1024]{1,0:T(8,128)(4,1)S(1)} %iota_compare_fusion, bf16[1024,512]{1,0:T(8,128)(2,1)S(1)} %copy-done), kind=kOutput, calls=%fused_computation.1 | convolution fusion | flops 1082130432 | bytes 11534336 | tf_op jit(solution)/shard_map/tho,sho->hts/dot_general | solution.py:53
  167.1 0.0 copy-done.6
  167.2 0.0 copy-done.2
  167.2 0.0 copy-start.1
  167.2 2.9 %fusion.15 = f32[4,1024,128]{1,2,0:T(8,128)S(1)} fusion(bf16[4,1024,1024]{2,1,0:T(8,128)(2,1)S(1)} %select_convert_fusion.1, bf16[1024,512]{1,0:T(8,128)(2,1)S(1)} %copy-done.2), kind=kOutput, calls=%fused_computation.24 | convolution fusion | flops 1073741824 | bytes 11534336 | tf_op jit(solution)/shard_map/ryx,xrj->yrj/dot_general | solution.py:61
  170.1 0.3 copy-done.1
  170.4 0.4 fusion.6
  170.8 1.5 copy.35
  172.3 7.2 %fusion.2 = f32[4,128,1024]{2,1,0:T(8,128)} fusion(bf16[1024,4,128]{0,2,1:T(8,128)(2,1)} %bitcast.105, pred[1024,1024]{1,0:T(8,128)(4,1)} %copy-done.6, bf16[1024,512]{1,0:T(8,128)(2,1)} %param.5, bf16[1024,512]{1,0:T(8,128)(2,1)S(1)} %copy-done.2), kind=kOutput, calls=%fused_computation.7 | convolution fusion | flops 2155872256 | bytes 6291456 | tf_op jit(solution)/shard_map/hts,tho->sho/dot_general | solution.py:67
  179.5 34.6 %all-gather.10.cloned.1.call-done = bf16[128,128,128]{2,1,0:T(8,128)(2,1)} async-done(((bf16[4,128,128]{2,1,0:T(8,128)(2,1)}), bf16[128,128,128]{2,1,0:T(8,128)(2,1)}) %all-gather.10.cloned.1.call-update) | async-done | bytes 4194320 | tf_op jit(solution)/shard_map/all_gather | solution.py:37
  214.2 0.0 copy-start.3
  214.2 0.0 copy-start.4
  214.2 3.4 %fusion = bf16[4,128,128]{2,1,0:T(8,128)(2,1)S(1)} fusion(bf16[32,4,128,128]{3,2,1,0:T(8,128)(2,1)} %bitcast.101, pred[32]{0:T(512)(128)(4,1)S(1)} %iota_compare_fusion.1), kind=kLoop, calls=%fused_computation.3 | loop fusion | flops 6225920 | bytes 4325408 | tf_op jit(solution)/shard_map/reduce_sum | solution.py:47
  217.6 0.4 fusion.18
  218.0 0.0 copy-done.3
  218.0 0.0 copy-done.4
  218.0 1.5 multiply_convert_fusion
  219.5 2.3 copy.37
  221.8 6.2 %fusion.4 = bf16[1024,4,128]{0,2,1:T(8,128)(2,1)} fusion(f32[4,128,1024]{2,1,0:T(8,128)S(1)} %fusion.18, bf16[4,1024,1024]{2,1,0:T(8,128)(2,1)} %copy-done.1, bf16[1024,512]{1,0:T(8,128)(2,1)} %param.5), kind=kOutput, calls=%fused_computation.10 | convolution fusion | flops 1075314688 | bytes 12582912 | tf_op jit(solution)/shard_map/hts,thq->shq/dot_general | solution.py:64
  228.0 2.3 copy.36
  (2 shorter events, 0.0 us)
Async XLA Ops:
  7.2 1.2 copy-start
  7.2 100.6 %all-gather.6.cloned.1.call-start = ((), (), s32[]{:S(2)}) async-start(), calls=%async_computation | async-start | bytes 9437184 | tf_op jit(solution)/shard_map/all_gather | solution.py:17
  7.9 153.1 %all-gather.8.cloned.1.call-start = ((), (), s32[]{:S(2)}) async-start(), calls=%async_computation.1 | async-start | bytes 4325376 | tf_op jit(solution)/shard_map/all_gather | solution.py:34
  10.8 107.0 %copy-start.5 = (bf16[1024,512]{1,0:T(8,128)(2,1)S(1)}, bf16[1024,512]{1,0:T(8,128)(2,1)}, u32[]{:S(2)}) copy-start(bf16[1024,512]{1,0:T(8,128)(2,1)} %param.5) | copy-start | bytes 3145732
  10.8 203.4 %all-gather.10.cloned.1.call-start = ((), (), s32[]{:S(2)}) async-start(), calls=%async_computation.2 | async-start | bytes 4325376 | tf_op jit(solution)/shard_map/all_gather | solution.py:37
  116.8 1.0 copy-start.7
  119.4 47.7 %copy-start.6 = (pred[1024,1024]{1,0:T(8,128)(4,1)}, pred[1024,1024]{1,0:T(8,128)(4,1)S(1)}, u32[]{:S(2)}) copy-start(pred[1024,1024]{1,0:T(8,128)(4,1)S(1)} %iota_compare_fusion) | copy-start | bytes 3145732
  161.1 3.3 %copy-start.8 = (bf16[1024,512]{0,1:T(8,128)(2,1)S(1)}, bf16[1024,512]{0,1:T(8,128)(2,1)}, u32[]{:S(2)}) copy-start(bf16[1024,512]{0,1:T(8,128)(2,1)} %copy-done.7) | copy-start | bytes 3145732
  164.4 2.8 %copy-start.2 = (bf16[1024,512]{1,0:T(8,128)(2,1)S(1)}, bf16[1024,512]{1,0:T(8,128)(2,1)}, u32[]{:S(2)}) copy-start(bf16[1024,512]{1,0:T(8,128)(2,1)} %param.6) | copy-start | bytes 3145732
  167.2 3.2 %copy-start.1 = (bf16[4,1024,1024]{2,1,0:T(8,128)(2,1)}, bf16[4,1024,1024]{2,1,0:T(8,128)(2,1)S(1)}, u32[]{:S(2)}) copy-start(bf16[4,1024,1024]{2,1,0:T(8,128)(2,1)S(1)} %select_convert_fusion.1) | copy-start | bytes 25165828
  214.2 3.8 %copy-start.3 = (bf16[1024,512]{1,0:T(8,128)(2,1)S(1)}, bf16[1024,512]{1,0:T(8,128)(2,1)}, u32[]{:S(2)}) copy-start(bf16[1024,512]{1,0:T(8,128)(2,1)} %param.6) | copy-start | bytes 3145732
  214.2 3.8 %copy-start.4 = (f32[4,128,1024]{2,1,0:T(8,128)S(1)}, f32[4,128,1024]{2,1,0:T(8,128)}, u32[]{:S(2)}) copy-start(f32[4,128,1024]{2,1,0:T(8,128)} %fusion.2) | copy-start | bytes 6291460
Sparse Core Ops, SparseCore 0:
  9.8 97.8 all-gather.5
  110.9 50.1 all-gather.7
  163.6 50.5 all-gather.9
where the time goes:
time: 237 us
  waiting for transfers between devices  174 us (73%)
  matrix products  33.3 us (14%)
  between operations  13.9 us (6%)
  local copies, waits for them, and re-layouts  8.56 us (4%)
  other arithmetic  7.02 us (3%)
    all_gather x1, waiting for transfers between devices, on_device(): lax.all_gather(out_grad, 'head', axis=1, tiled=True)  96.9 us
    all_gather x1, waiting for transfers between devices, on_device(): lax.all_gather(key_running_state[None].astype(jnp.bfloat16), 'seq', axis=...  41.6 us
    all_gather x1, waiting for transfers between devices, on_device(): lax.all_gather(query_state[None].astype(jnp.bfloat16), 'seq', axis=0, til...  34.6 us
    dot_general x1, matrix products, on_device(): lax.dot_general(lax.all_gather(out_grad, 'head', axis=1, tiled=True), out...  9.09 us
    unnamed x21, local copies, waits for them, and re-layouts  7.79 us
    dot_general x1, matrix products, on_device(): jnp.einsum('hts,tho->sho', attn_scores, gradient_heads, preferred_element...  7.22 us
    dot_general x1, matrix products, on_device(): jnp.einsum('hts,thq->shq', score_gradient, query_h, preferred_element_typ...  6.24 us
  transfers between devices with their start and end apart: 3, of which 3 were waited for; matrix products, arithmetic and copies ran while one was open for 13% of the time, Pallas kernels for 0%

commit v1 on v0

v1 whole, which is shorter than its diff:
```python
import functools
import math

import jax
import jax.numpy as jnp
from jax import lax
from jax.experimental import pallas as pl
from jax.experimental.pallas import tpu as pltpu
from jax.sharding import PartitionSpec as P

HD = 128
CH = 128
LANES = 8
BF = jnp.bfloat16
F32 = jnp.float32
MESH = pl.DeviceIdType.MESH


def mm(a, b, dims):
    return lax.dot_general(a, b, (dims, ((), ())), preferred_element_type=F32)


NN = ((1,), (0,))
NT = ((1,), (1,))
TN = ((0,), (0,))


def kernel(
    factor, zs, rows_n, heads,
    q_hbm, k_hbm, v_hbm, x_hbm, w_hbm,
    qg_hbm, kg_hbm, vg_hbm,
    q, k, v, w, xbuf, g, qg, kacc, vacc, kst, qst, qst_b, kgb, vgb,
    pre, suf, in1, in2, tot, out3,
    load_sem, store_sem, zsend, zrecv, s1, r1, s2, r2, s3, r3,
):
    tok = q.shape[0]
    width = x_hbm.shape[1]
    half = width // 2
    chunks = tok // CH
    z = lax.axis_index("head")
    seq = lax.axis_index("seq")
    lane = lax.rem(seq, LANES)
    row = seq // LANES
    right = lax.rem(z + 1, zs)
    left = lax.rem(z + zs - 1, zs)
    hops = zs // 2

    def seq_of(r, e):
        return r * LANES + e

    loads = [
        pltpu.make_async_copy(x_hbm, xbuf.at[z], load_sem.at[0]),
        pltpu.make_async_copy(k_hbm, k, load_sem.at[1]),
        pltpu.make_async_copy(v_hbm, v, load_sem.at[2]),
        pltpu.make_async_copy(w_hbm, w, load_sem.at[3]),
        pltpu.make_async_copy(q_hbm, q, load_sem.at[4]),
    ]
    for c in loads:
        c.start()

    barrier = pltpu.get_barrier_semaphore()
    for n in (left, right):
        pl.semaphore_signal(barrier, inc=1, device_id={"head": n}, device_id_type=MESH)
    for d in range(1, LANES):
        pl.semaphore_signal(
            barrier, inc=1, device_id={"seq": seq_of(row, lax.rem(lane + d, LANES))}, device_id_type=MESH
        )
    for d in range(1, rows_n):
        pl.semaphore_signal(
            barrier, inc=1, device_id={"seq": seq_of(lax.rem(row + d, rows_n), lane)}, device_id_type=MESH
        )
    pl.semaphore_wait(barrier, 2 + (LANES - 1) + (rows_n - 1))

    def ring(c, h):
        rows = pl.ds(pl.multiple_of(c * CH, CH), CH)
        copies = []
        for way, (to, sign) in enumerate(((right, -1), (left, 1))):
            src = lax.rem(z + zs + sign * (h - 1), zs)
            if h < hops:
                piece = xbuf.at[src, rows, :]
            else:
                piece = xbuf.at[src, rows, pl.ds(way * half, half)]
            copies.append(
                pltpu.make_async_remote_copy(
                    src_ref=piece,
                    dst_ref=piece,
                    send_sem=zsend.at[way, h - 1, c],
                    recv_sem=zrecv.at[way, h - 1, c],
                    device_id={"head": to},
                    device_id_type=MESH,
                )
            )
        return copies

    def send(c, h):
        for cp in ring(c, h):
            cp.start()

    def arrived(c, h):
        for cp in ring(c, h):
            cp.wait_recv()

    sl = heads * HD // LANES

    def ex1(which, st, d):
        to = lax.rem(lane + d, LANES)
        return pltpu.make_async_remote_copy(
            src_ref=st.at[pl.ds(pl.multiple_of(to * sl, sl), sl), :],
            dst_ref=in1.at[which, lane],
            send_sem=s1.at[which, d],
            recv_sem=r1.at[which, d],
            device_id={"seq": seq_of(row, to)},
            device_id_type=MESH,
        )

    def ex2(which, d):
        return pltpu.make_async_remote_copy(
            src_ref=tot.at[which],
            dst_ref=in2.at[which, row],
            send_sem=s2.at[which, d],
            recv_sem=r2.at[which, d],
            device_id={"seq": seq_of(lax.rem(row + d, rows_n), lane)},
            device_id_type=MESH,
        )

    def ex3(which, fin, d):
        to = lax.rem(lane + d, LANES)
        return pltpu.make_async_remote_copy(
            src_ref=out3.at[which, to],
            dst_ref=fin.at[pl.ds(pl.multiple_of(lane * sl, sl), sl), :],
            send_sem=s3.at[which, d],
            recv_sem=r3.at[which, d],
            device_id={"seq": seq_of(row, to)},
            device_id_type=MESH,
        )

    def phase1(which, st):
        for d in range(1, LANES):
            ex1(which, st, d).start()
        in1[which, lane] = st[pl.ds(pl.multiple_of(lane * sl, sl), sl), :]

    def phase2(which, st):
        for d in range(1, LANES):
            ex1(which, st, d).wait_recv()
        total = in1[which, 0].astype(F32)
        for e in range(1, LANES):
            total = total + in1[which, e].astype(F32)
        tot[which] = total
        for d in range(1, rows_n):
            ex2(which, d).start()

    def phase3(which, fin):
        for d in range(1, rows_n):
            ex2(which, d).wait_recv()
        in2[which, row] = jnp.zeros((sl, HD), F32)
        run = jnp.zeros((sl, HD), F32)
        for r in range(rows_n):
            keep = (r < row) if which == 0 else (r > row)
            run = run + jnp.where(keep, in2[which, r], 0.0)
        for e in range(LANES) if which == 0 else reversed(range(LANES)):
            out3[which, e] = run.astype(BF)
            run = run + in1[which, e].astype(F32)
        for d in range(1, LANES):
            ex3(which, fin, d).start()
        fin[pl.ds(pl.multiple_of(lane * sl, sl), sl), :] = out3[which, lane]

    def phase4(which, fin):
        for d in range(1, LANES):
            ex3(which, fin, d).wait_recv()

    def col(h):
        return pl.ds(h * HD, HD)

    def make_g(c):
        rows = pl.ds(pl.multiple_of(c * CH, CH), CH)
        x = jnp.concatenate([xbuf[s, rows, :] for s in range(zs)], axis=1)
        g[rows, :] = mm(x, w[...], NT).astype(BF)
        for h in range(heads):
            qst[col(h), :] += mm(q[rows, col(h)], g[rows, col(h)], TN)

    def head_part(c, h):
        rows = pl.ds(pl.multiple_of(c * CH, CH), CH)
        gc, qc = g[rows, col(h)], q[rows, col(h)]
        kh, vh = k[:, col(h)], v[:, col(h)]
        t = c * CH + lax.broadcasted_iota(jnp.int32, (CH, tok), 0)
        s = lax.broadcasted_iota(jnp.int32, (CH, tok), 1)
        sc = jnp.where(t >= s, mm(gc, vh, NT), 0.0).astype(BF)
        t2 = c * CH + lax.broadcasted_iota(jnp.int32, (tok, CH), 1)
        s2_ = lax.broadcasted_iota(jnp.int32, (tok, CH), 0)
        keep = t2 >= s2_
        sct = jnp.where(keep, mm(vh, gc, NT), 0.0).astype(BF)
        at = jnp.where(keep, mm(kh, qc, NT), 0.0).astype(BF)
        out = mm(sc, kh, NN) + mm(gc, pre[col(h), :], NT)
        qg[rows, col(h)] = (factor * out).astype(BF)
        kacc[:, col(h)] += mm(sct, qc, NN)
        vacc[:, col(h)] += mm(at, gc, NN)

    loads[0].wait()
    send(0, 1)
    send(1, 1)
    loads[1].wait()
    loads[2].wait()
    for h in range(heads):
        kst[col(h), :] = mm(k[:, col(h)], v[:, col(h)], TN).astype(BF)
    phase1(0, kst)
    kacc[...] = jnp.zeros_like(kacc)
    vacc[...] = jnp.zeros_like(vacc)
    qst[...] = jnp.zeros_like(qst)
    loads[3].wait()
    loads[4].wait()
    for h in range(2, hops + 1):
        for j in range(2):
            arrived(j, h - 1)
            send(j, h)
        if h == 2:
            phase2(0, kst)
        if h == 3:
            phase3(0, pre)
        if h == 4:
            phase4(0, pre)

    def pair(p, carry):
        a, b = 2 * p, 2 * p + 1
        send(a, 1)
        send(b, 1)
        arrived(a - 2, hops)
        make_g(a - 2)
        for h in range(2, hops + 1):
            for j, c in enumerate((a, b)):
                arrived(c, h - 1)
                send(c, h)
                if h == 2:
                    if j == 0:
                        head_part(a - 2, 0)
                        head_part(a - 2, 1)
                    else:
                        head_part(a - 2, 2)
                        head_part(a - 2, 3)
                if h == 3:
                    if j == 0:
                        arrived(b - 2, hops)
                        make_g(b - 2)
                    else:
                        head_part(b - 2, 0)
                        head_part(b - 2, 1)
                if h == 4 and j == 0:
                    head_part(b - 2, 2)
                    head_part(b - 2, 3)
        return carry

    lax.fori_loop(1, chunks // 2, pair, 0)
    a, b = chunks - 2, chunks - 1
    arrived(a, hops)
    make_g(a)
    arrived(b, hops)
    make_g(b)
    qst_b[...] = qst[...].astype(BF)
    phase1(1, qst_b)
    for h in range(heads):
        head_part(a, h)
    phase2(1, qst_b)
    head_part(b, 0)
    head_part(b, 1)
    phase3(1, suf)
    head_part(b, 2)
    head_part(b, 3)
    store_q = pltpu.make_async_copy(qg, qg_hbm, store_sem.at[0])
    store_q.start()
    phase4(1, suf)
    for h in range(heads):
        sh = suf[col(h), :]
        kgb[:, col(h)] = (factor * (kacc[:, col(h)] + mm(v[:, col(h)], sh, NT))).astype(BF)
    store_k = pltpu.make_async_copy(kgb, kg_hbm, store_sem.at[1])
    store_k.start()
    for h in range(heads):
        sh = suf[col(h), :]
        vgb[:, col(h)] = (factor * (vacc[:, col(h)] + mm(k[:, col(h)], sh, NN))).astype(BF)
    store_v = pltpu.make_async_copy(vgb, vg_hbm, store_sem.at[2])
    store_v.start()

    def drain(c, carry):
        for h in range(1, hops + 1):
            for cp in ring(c, h):
                cp.wait_send()
        return carry

    lax.fori_loop(0, chunks, drain, 0)
    for which, st, fin in ((0, kst, pre), (1, qst_b, suf)):
        for d in range(1, LANES):
            ex1(which, st, d).wait_send()
            ex3(which, fin, d).wait_send()
        for d in range(1, rows_n):
            ex2(which, d).wait_send()
    store_q.wait()
    store_k.wait()
    store_v.wait()


def on_device(queries, keys, values, out_grad, out_weight):
    tok, width = queries.shape
    zs = lax.axis_size("head")
    seqs = lax.axis_size("seq")
    heads = width // HD
    rows_n = seqs // LANES
    chunks = tok // CH
    sl = heads * HD // LANES
    factor = 1.0 / math.sqrt(HD * tok * seqs)
    out = jax.ShapeDtypeStruct((tok, width), BF)
    dma = pltpu.SemaphoreType.DMA
    return pl.pallas_call(
        functools.partial(kernel, factor, zs, rows_n, heads),
        out_shape=(out, out, out),
        in_specs=[pl.BlockSpec(memory_space=pl.ANY)] * 5,
        out_specs=[pl.BlockSpec(memory_space=pl.ANY)] * 3,
        scratch_shapes=[
            pltpu.VMEM((tok, width), BF),
            pltpu.VMEM((tok, width), BF),
            pltpu.VMEM((tok, width), BF),
            pltpu.VMEM((width, width * zs), BF),
            pltpu.VMEM((zs, tok, width), BF),
            pltpu.VMEM((tok, width), BF),
            pltpu.VMEM((tok, width), BF),
            pltpu.VMEM((tok, width), F32),
            pltpu.VMEM((tok, width), F32),
            pltpu.VMEM((width, HD), BF),
            pltpu.VMEM((width, HD), F32),
            pltpu.VMEM((width, HD), BF),
            pltpu.VMEM((tok, width), BF),
            pltpu.VMEM((tok, width), BF),
            pltpu.VMEM((width, HD), BF),
            pltpu.VMEM((width, HD), BF),
            pltpu.VMEM((2, LANES, sl, HD), BF),
            pltpu.VMEM((2, rows_n, sl, HD), F32),
            pltpu.VMEM((2, sl, HD), F32),
            pltpu.VMEM((2, LANES, sl, HD), BF),
            dma((5,)),
            dma((3,)),
            dma((2, zs // 2, chunks)),
            dma((2, zs // 2, chunks)),
            dma((2, LANES)),
            dma((2, LANES)),
            dma((2, rows_n)),
            dma((2, rows_n)),
            dma((2, LANES)),
            dma((2, LANES)),
        ],
        compiler_params=pltpu.CompilerParams(
            collective_id=0, has_side_effects=True, vmem_limit_bytes=56 * 1024 * 1024
        ),
        cost_estimate=pl.CostEstimate(
            flops=2 * tok * width * width * zs + 12 * tok * tok * width,
            bytes_accessed=16 * 1024 * 1024,
            transcendentals=0,
        ),
    )(queries, keys, values, out_grad, out_weight)


def solution(mesh):
    placed = (
        P("seq", "head"),
        P("seq", "head"),
        P("seq", "head"),
        P("seq", "head"),
        P("head", None),
    )
    return jax.shard_map(
        on_device,
        mesh=mesh,
        in_specs=placed,
        out_specs=(P("seq", "head"), P("seq", "head"), P("seq", "head")),
        check_vma=False,
    )
```

time: 237 us -> 120 us (0.51)
  waiting for transfers between devices: 174 us -> 0 us
  Pallas kernels: 0 us -> 114 us
  matrix products: 33.3 us -> 0 us
  between operations: 13.9 us -> 0.65 us
  other arithmetic: 7.02 us -> 0 us
  local copies, waits for them, and re-layouts: 8.56 us -> 5.59 us
    all_gather x3 -> x0, waiting for transfers between devices: 173 us -> none  [the longest x1 96.9 us: on_device(): lax.all_gather(out_grad, 'head', axis=1, tiled=True)]
    pallas_call x0 -> x1, Pallas kernels: none -> 114 us  [on_device(): pl.pallas_call(functools.partial(kernel, factor, zs, rows_n, heads), out_...]
    dot_general x10 -> x0, matrix products: 33.3 us -> none  [the longest x1 9.09 us: on_device(): lax.dot_general(lax.all_gather(out_grad, 'head', axis=1, tiled=True), out...]
    reduce_sum x2 -> x0, other arithmetic: 6.7 us -> none  [the longest x1 3.38 us: on_device(): jnp.sum(jnp.where(keep_late, portions[1], 0.0), axis=0)]
    unnamed x21 -> x5, local copies, waits for them, and re-layouts: 7.79 us -> 5.59 us
  transfers between devices with their start and end apart: 3 -> 0, of which waited for: 3 -> 0; matrix products, arithmetic and copies ran while one was open for 13% -> 0% of each run, Pallas kernels for 0% -> 0%
where the time goes in v1:
time: 120 us
  Pallas kernels  114 us (95%)
  local copies, waits for them, and re-layouts  5.59 us (5%)
    pallas_call x1, Pallas kernels, on_device(): pl.pallas_call(functools.partial(kernel, factor, zs, rows_n, heads), out_...  114 us
    unnamed x5, local copies, waits for them, and re-layouts  5.59 us

profile of v1, /device:TPU:1, one launch (start us, length us, event | category | flops | bytes accessed | tf_op | source)
XLA Modules:
  0.0 120.3 jit_solution(10463300820987363302)
XLA Ops:
  0.6 114.0 %shard_map.76 = (bf16[1024,512]{1,0:T(8,128)(2,1)}, bf16[1024,512]{1,0:T(8,128)(2,1)}, bf16[1024,512]{1,0:T(8,128)(2,1)}) custom-call(bf16[1024,512]{1,0:T(8,128)(2,1)} %q_hbm.1, bf16[1024,512]{1,0:T(8,128)(2,1)} %k_hbm.1, bf16[1024,512]{1,0:T(8,128)(2,1)} %v_hbm.1, bf16[1024,512]{1,0:T(8,128)(2,1)} %x_hbm.1, bf16[512,4096]{1,0:T(8,128)(2,1)} %w_hbm.1), custom_call_target="tpu_custom_call" | custom-call | flops 10737418240 | bytes 16777216 | tf_op jit(solution)/shard_map/pallas_call | solution.py:310
  114.7 0.0 copy-start
  114.7 2.4 %copy.11 = bf16[1024,512]{1,0:T(8,128)(2,1)} copy(bf16[1024,512]{1,0:T(8,128)(2,1)} %get-tuple-element.6) | data formatting | bytes 2097152
  117.0 2.3 %copy.12 = bf16[1024,512]{1,0:T(8,128)(2,1)} copy(bf16[1024,512]{1,0:T(8,128)(2,1)} %get-tuple-element.7) | data formatting | bytes 2097152
  119.3 0.0 copy-done
  119.3 1.0 copy.13
Async XLA Ops:
  114.7 4.6 %copy-start = (bf16[1024,512]{1,0:T(8,128)(2,1)S(1)}, bf16[1024,512]{1,0:T(8,128)(2,1)}, u32[]{:S(2)}) copy-start(bf16[1024,512]{1,0:T(8,128)(2,1)} %get-tuple-element.8) | copy-start | bytes 3145732

commit v2 on v1

--- a/solution.py
+++ b/solution.py
@@ -10,6 +10,7 @@
 
 HD = 128
 CH = 128
+BLK = 256
 LANES = 8
 BF = jnp.bfloat16
 F32 = jnp.float32
@@ -28,10 +29,10 @@
 def kernel(
     factor, zs, rows_n, heads,
     q_hbm, k_hbm, v_hbm, x_hbm, w_hbm,
-    qg_hbm, kg_hbm, vg_hbm,
-    q, k, v, w, xbuf, g, qg, kacc, vacc, kst, qst, qst_b, kgb, vgb,
+    qg, kg, vg,
+    q, k, v, w, xbuf, g, kacc, vacc, kst, qst, qst_b,
     pre, suf, in1, in2, tot, out3,
-    load_sem, store_sem, zsend, zrecv, s1, r1, s2, r2, s3, r3,
+    load_sem, zsend, zrecv, s1, r1, s2, r2, s3, r3,
 ):
     tok = q.shape[0]
     width = x_hbm.shape[1]
@@ -171,112 +172,108 @@
     def col(h):
         return pl.ds(h * HD, HD)
 
-    def make_g(c):
-        rows = pl.ds(pl.multiple_of(c * CH, CH), CH)
+    def make_g(t0):
+        rows = pl.ds(t0, BLK)
         x = jnp.concatenate([xbuf[s, rows, :] for s in range(zs)], axis=1)
         g[rows, :] = mm(x, w[...], NT).astype(BF)
         for h in range(heads):
             qst[col(h), :] += mm(q[rows, col(h)], g[rows, col(h)], TN)
 
-    def head_part(c, h):
-        rows = pl.ds(pl.multiple_of(c * CH, CH), CH)
-        gc, qc = g[rows, col(h)], q[rows, col(h)]
-        kh, vh = k[:, col(h)], v[:, col(h)]
-        t = c * CH + lax.broadcasted_iota(jnp.int32, (CH, tok), 0)
-        s = lax.broadcasted_iota(jnp.int32, (CH, tok), 1)
-        sc = jnp.where(t >= s, mm(gc, vh, NT), 0.0).astype(BF)
-        t2 = c * CH + lax.broadcasted_iota(jnp.int32, (tok, CH), 1)
-        s2_ = lax.broadcasted_iota(jnp.int32, (tok, CH), 0)
-        keep = t2 >= s2_
-        sct = jnp.where(keep, mm(vh, gc, NT), 0.0).astype(BF)
-        at = jnp.where(keep, mm(kh, qc, NT), 0.0).astype(BF)
-        out = mm(sc, kh, NN) + mm(gc, pre[col(h), :], NT)
-        qg[rows, col(h)] = (factor * out).astype(BF)
-        kacc[:, col(h)] += mm(sct, qc, NN)
-        vacc[:, col(h)] += mm(at, gc, NN)
+    def head_part(h, t0, t1):
+        causal = lax.broadcasted_iota(jnp.int32, (BLK, BLK), 0) >= lax.broadcasted_iota(
+            jnp.int32, (BLK, BLK), 1
+        )
+        causal_t = lax.broadcasted_iota(jnp.int32, (BLK, BLK), 1) >= lax.broadcasted_iota(
+            jnp.int32, (BLK, BLK), 0
+        )
+        for s0 in range(0, t1, BLK):
+            first = max(s0, t0)
+            rows, here = pl.ds(first, t1 - first), pl.ds(s0, BLK)
+
+            def masked(a, s0=s0):
+                if s0 < t0:
+                    return a.astype(BF)
+                diag = jnp.where(causal_t, a[:, :BLK], 0.0)
+                if a.shape[1] > BLK:
+                    diag = jnp.concatenate([diag, a[:, BLK:]], axis=1)
+                return diag.astype(BF)
+
+            sct = masked(mm(v[here, col(h)], g[rows, col(h)], NT))
+            at = masked(mm(k[here, col(h)], q[rows, col(h)], NT))
+            kpart = mm(sct, q[rows, col(h)], NN)
+            vpart = mm(at, g[rows, col(h)], NN)
+            if s0 < t0:
+                kpart = kpart + kacc[here, col(h)]
+                vpart = vpart + vacc[here, col(h)]
+            kacc[here, col(h)] = kpart
+            vacc[here, col(h)] = vpart
+        for r0 in range(t0, t1, BLK):
+            rows, past = pl.ds(r0, BLK), pl.ds(0, r0 + BLK)
+            a = mm(g[rows, col(h)], v[past, col(h)], NT)
+            diag = jnp.where(causal, a[:, r0:], 0.0)
+            if r0:
+                diag = jnp.concatenate([a[:, :r0], diag], axis=1)
+            out = mm(diag.astype(BF), k[past, col(h)], NN) + mm(g[rows, col(h)], pre[col(h), :], NT)
+            qg[rows, col(h)] = (factor * out).astype(BF)
+
+    depth = chunks // 2
+    group = [(c, h) for h in range(1, hops + 1) for c in range(depth)]
+    mid = tok // 2
 
     loads[0].wait()
-    send(0, 1)
-    send(1, 1)
+    for c in range(depth):
+        send(c, 1)
     loads[1].wait()
     loads[2].wait()
     for h in range(heads):
         kst[col(h), :] = mm(k[:, col(h)], v[:, col(h)], TN).astype(BF)
     phase1(0, kst)
-    kacc[...] = jnp.zeros_like(kacc)
-    vacc[...] = jnp.zeros_like(vacc)
     qst[...] = jnp.zeros_like(qst)
     loads[3].wait()
     loads[4].wait()
-    for h in range(2, hops + 1):
-        for j in range(2):
-            arrived(j, h - 1)
-            send(j, h)
-        if h == 2:
-            phase2(0, kst)
-        if h == 3:
-            phase3(0, pre)
-        if h == 4:
-            phase4(0, pre)
-
-    def pair(p, carry):
-        a, b = 2 * p, 2 * p + 1
-        send(a, 1)
-        send(b, 1)
-        arrived(a - 2, hops)
-        make_g(a - 2)
-        for h in range(2, hops + 1):
-            for j, c in enumerate((a, b)):
-                arrived(c, h - 1)
-                send(c, h)
-                if h == 2:
-                    if j == 0:
-                        head_part(a - 2, 0)
-                        head_part(a - 2, 1)
-                    else:
-                        head_part(a - 2, 2)
-                        head_part(a - 2, 3)
-                if h == 3:
-                    if j == 0:
-                        arrived(b - 2, hops)
-                        make_g(b - 2)
-                    else:
-                        head_part(b - 2, 0)
-                        head_part(b - 2, 1)
-                if h == 4 and j == 0:
-                    head_part(b - 2, 2)
-                    head_part(b - 2, 3)
-        return carry
-
-    lax.fori_loop(1, chunks // 2, pair, 0)
-    a, b = chunks - 2, chunks - 1
-    arrived(a, hops)
-    make_g(a)
-    arrived(b, hops)
-    make_g(b)
+    for c, h in group[depth:]:
+        arrived(c, h - 1)
+        send(c, h)
+        if c == depth - 1:
+            if h == 2:
+                phase2(0, kst)
+            if h == 3:
+                phase3(0, pre)
+            if h == 4:
+                phase4(0, pre)
+    for c in range(depth):
+        send(depth + c, 1)
+    for c in range(depth):
+        arrived(c, hops)
+    work = []
+    for t0 in range(0, mid, BLK):
+        work.append(functools.partial(make_g, t0))
+    for h in range(heads):
+        work.append(functools.partial(head_part, h, 0, mid))
+    for c, h in group[depth:]:
+        arrived(depth + c, h - 1)
+        send(depth + c, h)
+        if work:
+            work.pop(0)()
+    for f in work:
+        f()
+    per = BLK // CH
+    for i in range(depth // per):
+        for c in range(i * per, (i + 1) * per):
+            arrived(depth + c, hops)
+        make_g(mid + i * BLK)
     qst_b[...] = qst[...].astype(BF)
     phase1(1, qst_b)
     for h in range(heads):
-        head_part(a, h)
-    phase2(1, qst_b)
-    head_part(b, 0)
-    head_part(b, 1)
+        head_part(h, mid, tok)
+        if h == heads // 2 - 1:
+            phase2(1, qst_b)
     phase3(1, suf)
-    head_part(b, 2)
-    head_part(b, 3)
-    store_q = pltpu.make_async_copy(qg, qg_hbm, store_sem.at[0])
-    store_q.start()
     phase4(1, suf)
     for h in range(heads):
         sh = suf[col(h), :]
-        kgb[:, col(h)] = (factor * (kacc[:, col(h)] + mm(v[:, col(h)], sh, NT))).astype(BF)
-    store_k = pltpu.make_async_copy(kgb, kg_hbm, store_sem.at[1])
-    store_k.start()
-    for h in range(heads):
-        sh = suf[col(h), :]
-        vgb[:, col(h)] = (factor * (vacc[:, col(h)] + mm(k[:, col(h)], sh, NN))).astype(BF)
-    store_v = pltpu.make_async_copy(vgb, vg_hbm, store_sem.at[2])
-    store_v.start()
+        kg[:, col(h)] = (factor * (kacc[:, col(h)] + mm(v[:, col(h)], sh, NT))).astype(BF)
+        vg[:, col(h)] = (factor * (vacc[:, col(h)] + mm(k[:, col(h)], sh, NN))).astype(BF)
 
     def drain(c, carry):
         for h in range(1, hops + 1):
@@ -291,9 +288,6 @@
             ex3(which, fin, d).wait_send()
         for d in range(1, rows_n):
             ex2(which, d).wait_send()
-    store_q.wait()
-    store_k.wait()
-    store_v.wait()
 
 
 def on_device(queries, keys, values, out_grad, out_weight):
@@ -305,13 +299,13 @@
     chunks = tok // CH
     sl = heads * HD // LANES
     factor = 1.0 / math.sqrt(HD * tok * seqs)
-    out = jax.ShapeDtypeStruct((tok, width), BF)
+    out = pltpu.VMEM((tok, width), BF)
     dma = pltpu.SemaphoreType.DMA
     return pl.pallas_call(
         functools.partial(kernel, factor, zs, rows_n, heads),
         out_shape=(out, out, out),
-        in_specs=[pl.BlockSpec(memory_space=pl.ANY)] * 5,
-        out_specs=[pl.BlockSpec(memory_space=pl.ANY)] * 3,
+        in_specs=[pl.BlockSpec(memory_space=pltpu.HBM)] * 5,
+        out_specs=[pl.BlockSpec(memory_space=pltpu.VMEM)] * 3,
         scratch_shapes=[
             pltpu.VMEM((tok, width), BF),
             pltpu.VMEM((tok, width), BF),
@@ -319,14 +313,11 @@
             pltpu.VMEM((width, width * zs), BF),
             pltpu.VMEM((zs, tok, width), BF),
             pltpu.VMEM((tok, width), BF),
-            pltpu.VMEM((tok, width), BF),
             pltpu.VMEM((tok, width), F32),
             pltpu.VMEM((tok, width), F32),
             pltpu.VMEM((width, HD), BF),
             pltpu.VMEM((width, HD), F32),
             pltpu.VMEM((width, HD), BF),
-            pltpu.VMEM((tok, width), BF),
-            pltpu.VMEM((tok, width), BF),
             pltpu.VMEM((width, HD), BF),
             pltpu.VMEM((width, HD), BF),
             pltpu.VMEM((2, LANES, sl, HD), BF),
@@ -334,7 +325,6 @@
             pltpu.VMEM((2, sl, HD), F32),
             pltpu.VMEM((2, LANES, sl, HD), BF),
             dma((5,)),
-            dma((3,)),
             dma((2, zs // 2, chunks)),
             dma((2, zs // 2, chunks)),
             dma((2, LANES)),
@@ -345,7 +335,7 @@
             dma((2, LANES)),
         ],
         compiler_params=pltpu.CompilerParams(
-            collective_id=0, has_side_effects=True, vmem_limit_bytes=56 * 1024 * 1024
+            collective_id=0, has_side_effects=True, vmem_limit_bytes=60 * 1024 * 1024
         ),
         cost_estimate=pl.CostEstimate(
             flops=2 * tok * width * width * zs + 12 * tok * tok * width,

time: 120 us -> 111 us (0.925)
  Pallas kernels: 114 us -> 107 us
  local copies, waits for them, and re-layouts: 5.59 us -> 2.91 us
    pallas_call x1, Pallas kernels: 114 us -> 107 us  [on_device(): pl.pallas_call(functools.partial(kernel, factor, zs, rows_n, heads), out_...]
    unnamed x5 -> x3, local copies, waits for them, and re-layouts: 5.59 us -> 2.91 us
where the time goes in v2:
time: 111 us
  Pallas kernels  107 us (96%)
  local copies, waits for them, and re-layouts  2.91 us (3%)
    pallas_call x1, Pallas kernels, on_device(): pl.pallas_call(functools.partial(kernel, factor, zs, rows_n, heads), out_...  107 us
    unnamed x3, local copies, waits for them, and re-layouts  2.91 us

profile of v2, /device:TPU:1, one launch (start us, length us, event | category | flops | bytes accessed | tf_op | source)
XLA Modules:
  0.0 111.0 jit_solution(586135788879415447)
XLA Ops:
  0.6 107.4 %shard_map.76 = (bf16[1024,512]{1,0:T(8,128)(2,1)S(1)}, bf16[1024,512]{1,0:T(8,128)(2,1)S(1)}, bf16[1024,512]{1,0:T(8,128)(2,1)S(1)}) custom-call(bf16[1024,512]{1,0:T(8,128)(2,1)} %q_hbm.1, bf16[1024,512]{1,0:T(8,128)(2,1)} %k_hbm.1, bf16[1024,512]{1,0:T(8,128)(2,1)} %v_hbm.1, bf16[1024,512]{1,0:T(8,128)(2,1)} %x_hbm.1, bf16[512,4096]{1,0:T(8,128)(2,1)} %w_hbm.1), custom_call_target="tpu_custom_call" | custom-call | flops 10737418240 | bytes 16777216 | tf_op jit(solution)/shard_map/pallas_call | solution.py:304
  108.0 1.0 copy.11
  109.0 1.0 copy.12
  110.0 1.0 copy.13

commit v3 on v2

--- a/solution.py
+++ b/solution.py
@@ -9,7 +9,7 @@
 from jax.sharding import PartitionSpec as P
 
 HD = 128
-CH = 128
+CH = 64
 BLK = 256
 LANES = 8
 BF = jnp.bfloat16
@@ -30,38 +30,42 @@
     factor, zs, rows_n, heads,
     q_hbm, k_hbm, v_hbm, x_hbm, w_hbm,
     qg, kg, vg,
-    q, k, v, w, xbuf, g, kacc, vacc, kst, qst, qst_b,
+    q, k, v, w, xown, xq, gout, g, kacc, vacc, kst, qst, qst_b,
     pre, suf, in1, in2, tot, out3,
-    load_sem, zsend, zrecv, s1, r1, s2, r2, s3, r3,
+    load_sem, zsend, zrecv, fsend, frecv, wsend, wrecv, asend, arecv, bsend, brecv, dsend, drecv, csend, crecv, osend, orecv, s1, r1, s2, r2, s3, r3,
 ):
     tok = q.shape[0]
-    width = x_hbm.shape[1]
-    half = width // 2
-    chunks = tok // CH
+    quarter = tok // 4
+    subs = quarter // CH
     z = lax.axis_index("head")
     seq = lax.axis_index("seq")
     lane = lax.rem(seq, LANES)
     row = seq // LANES
-    right = lax.rem(z + 1, zs)
-    left = lax.rem(z + zs - 1, zs)
-    hops = zs // 2
+    y, x, c = row, lane // 2, lax.rem(lane, 2)
+    pair = z // 2
+    side = 2 * lax.rem(z, 2) - 1
+
+    def layer(n):
+        return lax.rem(z + zs + n * side, zs)
 
     def seq_of(r, e):
         return r * LANES + e
 
+    mine = pl.ds(pl.multiple_of(pair * quarter, quarter), quarter)
     loads = [
-        pltpu.make_async_copy(x_hbm, xbuf.at[z], load_sem.at[0]),
+        pltpu.make_async_copy(x_hbm, xown, load_sem.at[0]),
         pltpu.make_async_copy(k_hbm, k, load_sem.at[1]),
         pltpu.make_async_copy(v_hbm, v, load_sem.at[2]),
-        pltpu.make_async_copy(w_hbm, w, load_sem.at[3]),
-        pltpu.make_async_copy(q_hbm, q, load_sem.at[4]),
+        pltpu.make_async_copy(x_hbm.at[mine, :], xq.at[z], load_sem.at[3]),
+        pltpu.make_async_copy(w_hbm, w.at[0], load_sem.at[4]),
+        pltpu.make_async_copy(q_hbm, q, load_sem.at[5]),
     ]
-    for c in loads:
-        c.start()
+    for cp in loads:
+        cp.start()
 
     barrier = pltpu.get_barrier_semaphore()
-    for n in (left, right):
-        pl.semaphore_signal(barrier, inc=1, device_id={"head": n}, device_id_type=MESH)
+    for n in (1, -1, 2, -2, 3):
+        pl.semaphore_signal(barrier, inc=1, device_id={"head": layer(n)}, device_id_type=MESH)
     for d in range(1, LANES):
         pl.semaphore_signal(
             barrier, inc=1, device_id={"seq": seq_of(row, lax.rem(lane + d, LANES))}, device_id_type=MESH
@@ -70,36 +74,86 @@
         pl.semaphore_signal(
             barrier, inc=1, device_id={"seq": seq_of(lax.rem(row + d, rows_n), lane)}, device_id_type=MESH
         )
-    pl.semaphore_wait(barrier, 2 + (LANES - 1) + (rows_n - 1))
-
-    def ring(c, h):
-        rows = pl.ds(pl.multiple_of(c * CH, CH), CH)
-        copies = []
-        for way, (to, sign) in enumerate(((right, -1), (left, 1))):
-            src = lax.rem(z + zs + sign * (h - 1), zs)
-            if h < hops:
-                piece = xbuf.at[src, rows, :]
-            else:
-                piece = xbuf.at[src, rows, pl.ds(way * half, half)]
-            copies.append(
-                pltpu.make_async_remote_copy(
-                    src_ref=piece,
-                    dst_ref=piece,
-                    send_sem=zsend.at[way, h - 1, c],
-                    recv_sem=zrecv.at[way, h - 1, c],
-                    device_id={"head": to},
-                    device_id_type=MESH,
-                )
-            )
-        return copies
-
-    def send(c, h):
-        for cp in ring(c, h):
-            cp.start()
-
-    def arrived(c, h):
-        for cp in ring(c, h):
-            cp.wait_recv()
+    pl.semaphore_wait(barrier, 5 + (LANES - 1) + (rows_n - 1))
+
+    def remote(ref, dst, send_sem, recv_sem, to):
+        return pltpu.make_async_remote_copy(
+            src_ref=ref, dst_ref=dst, send_sem=send_sem, recv_sem=recv_sem, device_id=to, device_id_type=MESH
+        )
+
+    def x_first(i, n):
+        to = layer((1, -2, 3, -1)[i])
+        rows = pl.ds(pl.multiple_of(to // 2 * quarter + n * CH, CH), CH)
+        return remote(
+            xown.at[rows, :], xq.at[z, pl.ds(n * CH, CH), :], zsend.at[i, n], zrecv.at[i, n], {"head": to}
+        )
+
+    def x_relay(i, n):
+        piece = xq.at[layer(i + 1), pl.ds(n * CH, CH), :]
+        return remote(piece, piece, fsend.at[i, n], frecv.at[i, n], {"head": layer(-1)})
+
+    def w_z(b):
+        return remote(
+            w_hbm.at[y, x, c], w.at[b, y, x, c], wsend.at[b - 1], wrecv.at[b - 1], {"head": layer((1, -2, 3)[b - 1])}
+        )
+
+    half = x_hbm.shape[1] * zs // 2
+
+    def w_first(b, part, d):
+        piece = w.at[b, y, x, c, :, pl.ds(part * half, half)]
+        to = seq_of(y, lax.rem(lane + 2 * d, LANES)) if part == 0 else seq_of(lax.rem(y + d, rows_n), lane)
+        return remote(piece, piece, asend.at[b - 1, part, d - 1], arecv.at[b - 1, part, d - 1], {"seq": to})
+
+    def w_line(b, part, n, cols):
+        if part == 0:
+            return w.at[b, lax.rem(y + n, rows_n), :, c, :, cols]
+        return w.at[b, :, lax.rem(x + n, LANES // 2), c, :, cols]
+
+    def w_next(part, n):
+        if part == 0:
+            return {"seq": seq_of(lax.rem(y + n, rows_n), lane)}
+        return {"seq": seq_of(y, lax.rem(lane + 2 * n, LANES))}
+
+    def w_second(b, part, way):
+        piece = w_line(b, part, 0, pl.ds(part * half, half))
+        return remote(
+            piece, piece, bsend.at[b - 1, part, way], brecv.at[b - 1, part, way], w_next(part, (1, 3)[way])
+        )
+
+    def w_third(b, part, way):
+        piece = w_line(b, part, (3, 1)[way], pl.ds(part * half + way * (half // 2), half // 2))
+        return remote(
+            piece, piece, dsend.at[b - 1, part, way], drecv.at[b - 1, part, way], w_next(part, (1, 3)[way])
+        )
+
+    def w_core(b):
+        piece = w.at[b, :, :, c]
+        return remote(piece, piece, csend.at[b - 1], crecv.at[b - 1], {"seq": seq_of(y, 2 * x + 1 - c)})
+
+    def g_back(b):
+        return remote(
+            gout.at[b - 1], g.at[mine, :], osend.at[b - 1], orecv.at[b - 1], {"head": layer(b)}
+        )
+
+    ring3 = [(part, d) for part in range(2) for d in range(1, rows_n)]
+    ways = [(part, way) for part in range(2) for way in range(2)]
+
+    def start(make, b, keys):
+        for key in keys:
+            make(b, *key).start()
+
+    def wait(make, b, keys):
+        for key in keys:
+            make(b, *key).wait_recv()
+
+    def x_send(n):
+        for i in (2, 1, 0, 3):
+            x_first(i, n).start()
+
+    def x_pass(n):
+        for i in range(3):
+            x_first(i, n).wait_recv()
+            x_relay(i, n).start()
 
     sl = heads * HD // LANES
 
@@ -172,10 +226,12 @@
     def col(h):
         return pl.ds(h * HD, HD)
 
-    def make_g(t0):
-        rows = pl.ds(t0, BLK)
-        x = jnp.concatenate([xbuf[s, rows, :] for s in range(zs)], axis=1)
-        g[rows, :] = mm(x, w[...], NT).astype(BF)
+    def product(b):
+        xs = jnp.concatenate([xq[s] for s in range(zs)], axis=1)
+        wb = w[b].reshape(x_hbm.shape[1], x_hbm.shape[1] * zs)
+        return mm(xs, wb, NT).astype(BF)
+
+    def add_state(rows):
         for h in range(heads):
             qst[col(h), :] += mm(q[rows, col(h)], g[rows, col(h)], TN)
 
@@ -216,72 +272,93 @@
             out = mm(diag.astype(BF), k[past, col(h)], NN) + mm(g[rows, col(h)], pre[col(h), :], NT)
             qg[rows, col(h)] = (factor * out).astype(BF)
 
-    depth = chunks // 2
-    group = [(c, h) for h in range(1, hops + 1) for c in range(depth)]
-    mid = tok // 2
-
+    for b in (3, 2, 1):
+        w_z(b).start()
     loads[0].wait()
-    for c in range(depth):
-        send(c, 1)
+    x_send(0)
     loads[1].wait()
     loads[2].wait()
     for h in range(heads):
         kst[col(h), :] = mm(k[:, col(h)], v[:, col(h)], TN).astype(BF)
     phase1(0, kst)
     qst[...] = jnp.zeros_like(qst)
-    loads[3].wait()
-    loads[4].wait()
-    for c, h in group[depth:]:
-        arrived(c, h - 1)
-        send(c, h)
-        if c == depth - 1:
-            if h == 2:
-                phase2(0, kst)
-            if h == 3:
-                phase3(0, pre)
-            if h == 4:
-                phase4(0, pre)
-    for c in range(depth):
-        send(depth + c, 1)
-    for c in range(depth):
-        arrived(c, hops)
-    work = []
-    for t0 in range(0, mid, BLK):
-        work.append(functools.partial(make_g, t0))
-    for h in range(heads):
-        work.append(functools.partial(head_part, h, 0, mid))
-    for c, h in group[depth:]:
-        arrived(depth + c, h - 1)
-        send(depth + c, h)
-        if work:
-            work.pop(0)()
-    for f in work:
-        f()
-    per = BLK // CH
-    for i in range(depth // per):
-        for c in range(i * per, (i + 1) * per):
-            arrived(depth + c, hops)
-        make_g(mid + i * BLK)
+    for b in (3, 2, 1):
+        w_z(b).wait_recv()
+        start(w_first, b, ring3)
+        x_send(4 - b)
+    wait(w_first, 3, ring3)
+    start(w_second, 3, ways)
+    x_pass(0)
+    phase2(0, kst)
+    wait(w_first, 2, ring3)
+    wait(w_first, 1, ring3)
+    x_pass(1)
+    phase3(0, pre)
+    wait(w_second, 3, ways)
+    start(w_third, 3, ways)
+    start(w_second, 2, ways)
+    x_pass(2)
+    phase4(0, pre)
+    wait(w_third, 3, ways)
+    w_core(3).start()
+    wait(w_second, 2, ways)
+    start(w_third, 2, ways)
+    start(w_second, 1, ways)
+    x_pass(3)
+    for n in range(subs):
+        x_first(3, n).wait_recv()
+        for i in range(3):
+            x_relay(i, n).wait_recv()
+    for cp in loads[3:]:
+        cp.wait()
+    w_core(3).wait_recv()
+    gout[2] = product(3)
+    g_back(3).start()
+    wait(w_third, 2, ways)
+    w_core(2).start()
+    wait(w_second, 1, ways)
+    start(w_third, 1, ways)
+    g[mine, :] = product(0)
+    add_state(mine)
+    w_core(2).wait_recv()
+    gout[1] = product(2)
+    g_back(2).start()
+    wait(w_third, 1, ways)
+    w_core(1).start()
+    w_core(1).wait_recv()
+    gout[0] = product(1)
+    g_back(1).start()
+    for b in (3, 2, 1):
+        g_back(b).wait_recv()
+        add_state(pl.ds(pl.multiple_of(layer((1, -2, 3)[b - 1]) // 2 * quarter, quarter), quarter))
     qst_b[...] = qst[...].astype(BF)
     phase1(1, qst_b)
     for h in range(heads):
-        head_part(h, mid, tok)
-        if h == heads // 2 - 1:
+        head_part(h, 0, tok)
+        if h == 1:
             phase2(1, qst_b)
-    phase3(1, suf)
+        if h == 2:
+            phase3(1, suf)
     phase4(1, suf)
     for h in range(heads):
         sh = suf[col(h), :]
         kg[:, col(h)] = (factor * (kacc[:, col(h)] + mm(v[:, col(h)], sh, NT))).astype(BF)
         vg[:, col(h)] = (factor * (vacc[:, col(h)] + mm(k[:, col(h)], sh, NN))).astype(BF)
 
-    def drain(c, carry):
-        for h in range(1, hops + 1):
-            for cp in ring(c, h):
-                cp.wait_send()
-        return carry
-
-    lax.fori_loop(0, chunks, drain, 0)
+    for n in range(subs):
+        for i in range(4):
+            x_first(i, n).wait_send()
+        for i in range(3):
+            x_relay(i, n).wait_send()
+    for b in range(1, 4):
+        w_z(b).wait_send()
+        for key in ring3:
+            w_first(b, *key).wait_send()
+        for key in ways:
+            w_second(b, *key).wait_send()
+            w_third(b, *key).wait_send()
+        w_core(b).wait_send()
+        g_back(b).wait_send()
     for which, st, fin in ((0, kst, pre), (1, qst_b, suf)):
         for d in range(1, LANES):
             ex1(which, st, d).wait_send()
@@ -296,10 +373,11 @@
     seqs = lax.axis_size("seq")
     heads = width // HD
     rows_n = seqs // LANES
-    chunks = tok // CH
+    subs = tok // 4 // CH
     sl = heads * HD // LANES
     factor = 1.0 / math.sqrt(HD * tok * seqs)
     out = pltpu.VMEM((tok, width), BF)
+    slices = out_weight.reshape(rows_n, LANES // 2, 2, width // seqs, width * zs)
     dma = pltpu.SemaphoreType.DMA
     return pl.pallas_call(
         functools.partial(kernel, factor, zs, rows_n, heads),
@@ -310,8 +388,10 @@
             pltpu.VMEM((tok, width), BF),
             pltpu.VMEM((tok, width), BF),
             pltpu.VMEM((tok, width), BF),
-            pltpu.VMEM((width, width * zs), BF),
-            pltpu.VMEM((zs, tok, width), BF),
+            pltpu.VMEM((4, rows_n, LANES // 2, 2, width // seqs, width * zs), BF),
+            pltpu.VMEM((tok, width), BF),
+            pltpu.VMEM((zs, tok // 4, width), BF),
+            pltpu.VMEM((3, tok // 4, width), BF),
             pltpu.VMEM((tok, width), BF),
             pltpu.VMEM((tok, width), F32),
             pltpu.VMEM((tok, width), F32),
@@ -324,9 +404,23 @@
             pltpu.VMEM((2, rows_n, sl, HD), F32),
             pltpu.VMEM((2, sl, HD), F32),
             pltpu.VMEM((2, LANES, sl, HD), BF),
-            dma((5,)),
-            dma((2, zs // 2, chunks)),
-            dma((2, zs // 2, chunks)),
+            dma((6,)),
+            dma((4, subs)),
+            dma((4, subs)),
+            dma((3, subs)),
+            dma((3, subs)),
+            dma((3,)),
+            dma((3,)),
+            dma((3, 2, rows_n - 1)),
+            dma((3, 2, rows_n - 1)),
+            dma((3, 2, 2)),
+            dma((3, 2, 2)),
+            dma((3, 2, 2)),
+            dma((3, 2, 2)),
+            dma((3,)),
+            dma((3,)),
+            dma((3,)),
+            dma((3,)),
             dma((2, LANES)),
             dma((2, LANES)),
             dma((2, rows_n)),
@@ -342,7 +436,7 @@
             bytes_accessed=16 * 1024 * 1024,
             transcendentals=0,
         ),
-    )(queries, keys, values, out_grad, out_weight)
+    )(queries, keys, values, out_grad, slices)
 
 
 def solution(mesh):

time: 111 us -> 99.4 us (0.90)
  Pallas kernels: 107 us -> 95.8 us
    pallas_call x1, Pallas kernels: 107 us -> 95.8 us  [on_device(): pl.pallas_call(functools.partial(kernel, factor, zs, rows_n, heads), out_...]
where the time goes in v3:
time: 99.4 us; the launch traced here: 99.3 us
  Pallas kernels  95.8 us (96%)
  local copies, waits for them, and re-layouts  2.91 us (3%)
    pallas_call x1, Pallas kernels, on_device(): pl.pallas_call(functools.partial(kernel, factor, zs, rows_n, heads), out_...  95.8 us
    unnamed x3, local copies, waits for them, and re-layouts  2.91 us

profile of v3, /device:TPU:1, one launch (start us, length us, event | category | flops | bytes accessed | tf_op | source)
XLA Modules:
  0.0 99.3 jit_solution(9167870405209518360)
XLA Ops:
  0.6 95.8 %shard_map.76 = (bf16[1024,512]{1,0:T(8,128)(2,1)S(1)}, bf16[1024,512]{1,0:T(8,128)(2,1)S(1)}, bf16[1024,512]{1,0:T(8,128)(2,1)S(1)}) custom-call(bf16[1024,512]{1,0:T(8,128)(2,1)} %q_hbm.1, bf16[1024,512]{1,0:T(8,128)(2,1)} %k_hbm.1, bf16[1024,512]{1,0:T(8,128)(2,1)} %v_hbm.1, bf16[1024,512]{1,0:T(8,128)(2,1)} %x_hbm.1, bf16[4,4,2,16,4096]{4,3,2,1,0:T(8,128)(2,1)} %bitcast.1), custom_call_target="tpu_custom_call" | custom-call | flops 10737418240 | bytes 16777216 | tf_op jit(solution)/shard_map/pallas_call | solution.py:382
  96.4 1.0 copy.11
  97.4 1.0 copy.12
  98.3 1.0 copy.13

commit v4 on v3

--- a/solution.py
+++ b/solution.py
@@ -11,6 +11,8 @@
 HD = 128
 CH = 64
 BLK = 256
+AT2 = 13
+AT3 = 24
 LANES = 8
 BF = jnp.bfloat16
 F32 = jnp.float32
@@ -29,11 +31,12 @@
 def kernel(
     factor, zs, rows_n, heads,
     q_hbm, k_hbm, v_hbm, x_hbm, w_hbm,
-    qg, kg, vg,
+    res,
     q, k, v, w, xown, xq, gout, g, kacc, vacc, kst, qst, qst_b,
     pre, suf, in1, in2, tot, out3,
     load_sem, zsend, zrecv, fsend, frecv, wsend, wrecv, asend, arecv, bsend, brecv, dsend, drecv, csend, crecv, osend, orecv, s1, r1, s2, r2, s3, r3,
 ):
+    qg, kg, vg = res.at[0], res.at[1], res.at[2]
     tok = q.shape[0]
     quarter = tok // 4
     subs = quarter // CH
@@ -94,20 +97,20 @@
 
     def w_z(b):
         return remote(
-            w_hbm.at[y, x, c], w.at[b, y, x, c], wsend.at[b - 1], wrecv.at[b - 1], {"head": layer((1, -2, 3)[b - 1])}
+            w_hbm.at[c, y, x], w.at[b, c, y, x], wsend.at[b - 1], wrecv.at[b - 1], {"head": layer((1, -2, 3)[b - 1])}
         )
 
     half = x_hbm.shape[1] * zs // 2
 
     def w_first(b, part, d):
-        piece = w.at[b, y, x, c, :, pl.ds(part * half, half)]
+        piece = w.at[b, c, y, x, :, pl.ds(part * half, half)]
         to = seq_of(y, lax.rem(lane + 2 * d, LANES)) if part == 0 else seq_of(lax.rem(y + d, rows_n), lane)
         return remote(piece, piece, asend.at[b - 1, part, d - 1], arecv.at[b - 1, part, d - 1], {"seq": to})
 
     def w_line(b, part, n, cols):
         if part == 0:
-            return w.at[b, lax.rem(y + n, rows_n), :, c, :, cols]
-        return w.at[b, :, lax.rem(x + n, LANES // 2), c, :, cols]
+            return w.at[b, c, lax.rem(y + n, rows_n), :, :, cols]
+        return w.at[b, c, :, lax.rem(x + n, LANES // 2), :, cols]
 
     def w_next(part, n):
         if part == 0:
@@ -126,15 +129,26 @@
             piece, piece, dsend.at[b - 1, part, way], drecv.at[b - 1, part, way], w_next(part, (1, 3)[way])
         )
 
-    def w_core(b):
-        piece = w.at[b, :, :, c]
-        return remote(piece, piece, csend.at[b - 1], crecv.at[b - 1], {"seq": seq_of(y, 2 * x + 1 - c)})
-
-    def g_back(b):
-        return remote(
-            gout.at[b - 1], g.at[mine, :], osend.at[b - 1], orecv.at[b - 1], {"head": layer(b)}
-        )
-
+    def w_core(b, part, n):
+        piece = w_line(b, part, n, pl.ds(part * half, half))
+        return remote(
+            piece, piece, csend.at[b - 1, part, n], crecv.at[b - 1, part, n], {"seq": seq_of(y, 2 * x + 1 - c)}
+        )
+
+    span = x_hbm.shape[1] // 2
+
+    def of_core(core):
+        return pl.ds(pl.multiple_of(core * span, span), span)
+
+    def g_back(b, i):
+        core = lax.rem(c + i, 2)
+        return remote(
+            gout.at[b - 1, :, of_core(core)], g.at[mine, of_core(core)], osend.at[b - 1, i], orecv.at[b - 1, i],
+            {"head": layer(b)},
+        )
+
+    near = [(part, n) for part in range(2) for n in (0, 1, 3)]
+    far = [(part, 2) for part in range(2)]
     ring3 = [(part, d) for part in range(2) for d in range(1, rows_n)]
     ways = [(part, way) for part in range(2) for way in range(2)]
 
@@ -226,44 +240,46 @@
     def col(h):
         return pl.ds(h * HD, HD)
 
-    def product(b):
-        xs = jnp.concatenate([xq[s] for s in range(zs)], axis=1)
-        wb = w[b].reshape(x_hbm.shape[1], x_hbm.shape[1] * zs)
+    def product(b, core):
+        xs = jnp.concatenate([xq[i] for i in range(zs)], axis=1)
+        wb = w[b, core].reshape(span, x_hbm.shape[1] * zs)
         return mm(xs, wb, NT).astype(BF)
 
-    def add_state(rows):
-        for h in range(heads):
-            qst[col(h), :] += mm(q[rows, col(h)], g[rows, col(h)], TN)
-
-    def head_part(h, t0, t1):
+    def g_part(b, i):
+        core = lax.rem(c + i, 2)
+        if b == 0:
+            g[mine, of_core(core)] = product(b, core)
+        else:
+            gout[b - 1, :, of_core(core)] = product(b, core)
+            g_back(b, i).start()
+
+    def add_state(rows, core):
+        for i in range(heads // 2):
+            here = pl.ds(pl.multiple_of(core * span + i * HD, HD), HD)
+            qst[here, :] += mm(q[rows, here], g[rows, here], TN)
+
+    def head_parts(h):
         causal = lax.broadcasted_iota(jnp.int32, (BLK, BLK), 0) >= lax.broadcasted_iota(
             jnp.int32, (BLK, BLK), 1
         )
         causal_t = lax.broadcasted_iota(jnp.int32, (BLK, BLK), 1) >= lax.broadcasted_iota(
             jnp.int32, (BLK, BLK), 0
         )
-        for s0 in range(0, t1, BLK):
-            first = max(s0, t0)
-            rows, here = pl.ds(first, t1 - first), pl.ds(s0, BLK)
-
-            def masked(a, s0=s0):
-                if s0 < t0:
-                    return a.astype(BF)
-                diag = jnp.where(causal_t, a[:, :BLK], 0.0)
-                if a.shape[1] > BLK:
-                    diag = jnp.concatenate([diag, a[:, BLK:]], axis=1)
-                return diag.astype(BF)
-
+
+        def masked(a):
+            diag = jnp.where(causal_t, a[:, :BLK], 0.0)
+            if a.shape[1] > BLK:
+                diag = jnp.concatenate([diag, a[:, BLK:]], axis=1)
+            return diag.astype(BF)
+
+        def kv_part(s0):
+            rows, here = pl.ds(s0, tok - s0), pl.ds(s0, BLK)
             sct = masked(mm(v[here, col(h)], g[rows, col(h)], NT))
+            kacc[here, col(h)] = mm(sct, q[rows, col(h)], NN)
             at = masked(mm(k[here, col(h)], q[rows, col(h)], NT))
-            kpart = mm(sct, q[rows, col(h)], NN)
-            vpart = mm(at, g[rows, col(h)], NN)
-            if s0 < t0:
-                kpart = kpart + kacc[here, col(h)]
-                vpart = vpart + vacc[here, col(h)]
-            kacc[here, col(h)] = kpart
-            vacc[here, col(h)] = vpart
-        for r0 in range(t0, t1, BLK):
+            vacc[here, col(h)] = mm(at, g[rows, col(h)], NN)
+
+        def q_part(r0):
             rows, past = pl.ds(r0, BLK), pl.ds(0, r0 + BLK)
             a = mm(g[rows, col(h)], v[past, col(h)], NT)
             diag = jnp.where(causal, a[:, r0:], 0.0)
@@ -271,6 +287,9 @@
                 diag = jnp.concatenate([a[:, :r0], diag], axis=1)
             out = mm(diag.astype(BF), k[past, col(h)], NN) + mm(g[rows, col(h)], pre[col(h), :], NT)
             qg[rows, col(h)] = (factor * out).astype(BF)
+
+        parts = [functools.partial(kv_part, s0) for s0 in range(0, tok, BLK)]
+        return parts + [functools.partial(q_part, r0) for r0 in range(0, tok, BLK)]
 
     for b in (3, 2, 1):
         w_z(b).start()
@@ -297,13 +316,15 @@
     wait(w_second, 3, ways)
     start(w_third, 3, ways)
     start(w_second, 2, ways)
+    start(w_core, 3, near)
     x_pass(2)
     phase4(0, pre)
     wait(w_third, 3, ways)
-    w_core(3).start()
+    start(w_core, 3, far)
     wait(w_second, 2, ways)
     start(w_third, 2, ways)
     start(w_second, 1, ways)
+    start(w_core, 2, near)
     x_pass(3)
     for n in range(subs):
         x_first(3, n).wait_recv()
@@ -311,34 +332,39 @@
             x_relay(i, n).wait_recv()
     for cp in loads[3:]:
         cp.wait()
-    w_core(3).wait_recv()
-    gout[2] = product(3)
-    g_back(3).start()
+    g_part(3, 0)
+    wait(w_core, 3, near + far)
+    g_part(3, 1)
     wait(w_third, 2, ways)
-    w_core(2).start()
+    start(w_core, 2, far)
+    g_part(2, 0)
     wait(w_second, 1, ways)
     start(w_third, 1, ways)
-    g[mine, :] = product(0)
-    add_state(mine)
-    w_core(2).wait_recv()
-    gout[1] = product(2)
-    g_back(2).start()
+    start(w_core, 1, near)
+    wait(w_core, 2, near + far)
+    g_part(2, 1)
+    g_part(0, 0)
+    g_part(0, 1)
+    add_state(mine, 0)
+    add_state(mine, 1)
     wait(w_third, 1, ways)
-    w_core(1).start()
-    w_core(1).wait_recv()
-    gout[0] = product(1)
-    g_back(1).start()
+    start(w_core, 1, far)
+    g_part(1, 0)
+    wait(w_core, 1, near + far)
+    g_part(1, 1)
     for b in (3, 2, 1):
-        g_back(b).wait_recv()
-        add_state(pl.ds(pl.multiple_of(layer((1, -2, 3)[b - 1]) // 2 * quarter, quarter), quarter))
+        rows = pl.ds(pl.multiple_of(layer((1, -2, 3)[b - 1]) // 2 * quarter, quarter), quarter)
+        for i in range(2):
+            g_back(b, i).wait_recv()
+            add_state(rows, lax.rem(c + i, 2))
     qst_b[...] = qst[...].astype(BF)
     phase1(1, qst_b)
-    for h in range(heads):
-        head_part(h, 0, tok)
-        if h == 1:
+    for i, part in enumerate(sum([head_parts(h) for h in range(heads)], [])):
+        if i == AT2:
             phase2(1, qst_b)
-        if h == 2:
+        if i == AT3:
             phase3(1, suf)
+        part()
     phase4(1, suf)
     for h in range(heads):
         sh = suf[col(h), :]
@@ -357,8 +383,10 @@
         for key in ways:
             w_second(b, *key).wait_send()
             w_third(b, *key).wait_send()
-        w_core(b).wait_send()
-        g_back(b).wait_send()
+        for key in near + far:
+            w_core(b, *key).wait_send()
+        for i in range(2):
+            g_back(b, i).wait_send()
     for which, st, fin in ((0, kst, pre), (1, qst_b, suf)):
         for d in range(1, LANES):
             ex1(which, st, d).wait_send()
@@ -376,19 +404,19 @@
     subs = tok // 4 // CH
     sl = heads * HD // LANES
     factor = 1.0 / math.sqrt(HD * tok * seqs)
-    out = pltpu.VMEM((tok, width), BF)
-    slices = out_weight.reshape(rows_n, LANES // 2, 2, width // seqs, width * zs)
+    out = pltpu.VMEM((3, tok, width), BF)
+    slices = out_weight.reshape(2, rows_n, LANES // 2, width // seqs, width * zs)
     dma = pltpu.SemaphoreType.DMA
-    return pl.pallas_call(
+    big = pl.pallas_call(
         functools.partial(kernel, factor, zs, rows_n, heads),
-        out_shape=(out, out, out),
+        out_shape=out,
         in_specs=[pl.BlockSpec(memory_space=pltpu.HBM)] * 5,
-        out_specs=[pl.BlockSpec(memory_space=pltpu.VMEM)] * 3,
+        out_specs=pl.BlockSpec(memory_space=pltpu.VMEM),
         scratch_shapes=[
             pltpu.VMEM((tok, width), BF),
             pltpu.VMEM((tok, width), BF),
             pltpu.VMEM((tok, width), BF),
-            pltpu.VMEM((4, rows_n, LANES // 2, 2, width // seqs, width * zs), BF),
+            pltpu.VMEM((4, 2, rows_n, LANES // 2, width // seqs, width * zs), BF),
             pltpu.VMEM((tok, width), BF),
             pltpu.VMEM((zs, tok // 4, width), BF),
             pltpu.VMEM((3, tok // 4, width), BF),
@@ -417,10 +445,10 @@
             dma((3, 2, 2)),
             dma((3, 2, 2)),
             dma((3, 2, 2)),
-            dma((3,)),
-            dma((3,)),
-            dma((3,)),
-            dma((3,)),
+            dma((3, 2, rows_n)),
+            dma((3, 2, rows_n)),
+            dma((3, 2)),
+            dma((3, 2)),
             dma((2, LANES)),
             dma((2, LANES)),
             dma((2, rows_n)),
@@ -437,6 +465,7 @@
             transcendentals=0,
         ),
     )(queries, keys, values, out_grad, slices)
+    return big[0], big[1], big[2]
 
 
 def solution(mesh):

time: 99.4 us -> 98.2 us (0.988)
  local copies, waits for them, and re-layouts: 2.91 us -> 1.73 us
    unnamed x3 -> x0, local copies, waits for them, and re-layouts: 2.91 us -> none
    squeeze x0 -> x1, local copies, waits for them, and re-layouts: none -> 1.73 us  [on_device(): return (big[0], big[1], big[2])]
where the time goes in v4:
time: 98.2 us; the launch traced here: 98.1 us
  Pallas kernels  95.7 us (97%)
  local copies, waits for them, and re-layouts  1.73 us (2%)
    pallas_call x1, Pallas kernels, on_device(): pl.pallas_call(functools.partial(kernel, factor, zs, rows_n, heads), out_...  95.7 us

profile of v4, /device:TPU:1, one launch (start us, length us, event | category | flops | bytes accessed | tf_op | source)
XLA Modules:
  0.0 98.1 jit_solution(978543018038866472)
XLA Ops:
  0.6 95.7 %shard_map.76 = bf16[3,1024,512]{2,1,0:T(8,128)(2,1)S(1)} custom-call(bf16[1024,512]{1,0:T(8,128)(2,1)} %q_hbm.1, bf16[1024,512]{1,0:T(8,128)(2,1)} %k_hbm.1, bf16[1024,512]{1,0:T(8,128)(2,1)} %v_hbm.1, bf16[1024,512]{1,0:T(8,128)(2,1)} %x_hbm.1, bf16[2,4,4,16,4096]{4,3,2,1,0:T(8,128)(2,1)} %bitcast.7), custom_call_target="tpu_custom_call" | custom-call | flops 10737418240 | bytes 16777216 | tf_op jit(solution)/shard_map/pallas_call | solution.py:410
  96.4 1.7 %slice_bitcast_fusion = (bf16[1024,512]{1,0:T(8,128)(2,1)}, bf16[1024,512]{1,0:T(8,128)(2,1)}, bf16[1024,512]{1,0:T(8,128)(2,1)}) fusion(bf16[3,1024,512]{2,1,0:T(8,128)(2,1)S(1)} %shard_map.76), kind=kLoop, calls=%fused_computation | loop fusion | bytes 6291456 | tf_op jit(solution)/shard_map/squeeze | solution.py:468

commit v5 on v4

--- a/solution.py
+++ b/solution.py
@@ -140,11 +140,14 @@
     def of_core(core):
         return pl.ds(pl.multiple_of(core * span, span), span)
 
-    def g_back(b, i):
+    part_rows = quarter // 2
+
+    def g_back(b, i, t):
         core = lax.rem(c + i, 2)
+        rows = pl.ds(pl.multiple_of(pair * quarter + t * part_rows, part_rows), part_rows)
         return remote(
-            gout.at[b - 1, :, of_core(core)], g.at[mine, of_core(core)], osend.at[b - 1, i], orecv.at[b - 1, i],
-            {"head": layer(b)},
+            gout.at[b - 1, pl.ds(t * part_rows, part_rows), of_core(core)], g.at[rows, of_core(core)],
+            osend.at[b - 1, i, t], orecv.at[b - 1, i, t], {"head": layer(b)},
         )
 
     near = [(part, n) for part in range(2) for n in (0, 1, 3)]
@@ -240,8 +243,8 @@
     def col(h):
         return pl.ds(h * HD, HD)
 
-    def product(b, core):
-        xs = jnp.concatenate([xq[i] for i in range(zs)], axis=1)
+    def product(b, core, rows=slice(None)):
+        xs = jnp.concatenate([xq[i, rows, :] for i in range(zs)], axis=1)
         wb = w[b, core].reshape(span, x_hbm.shape[1] * zs)
         return mm(xs, wb, NT).astype(BF)
 
@@ -251,7 +254,19 @@
             g[mine, of_core(core)] = product(b, core)
         else:
             gout[b - 1, :, of_core(core)] = product(b, core)
-            g_back(b, i).start()
+            for t in range(2):
+                g_back(b, i, t).start()
+
+    def g_half(b, i, t):
+        core, rows = lax.rem(c + i, 2), pl.ds(t * part_rows, part_rows)
+        gout[b - 1, rows, of_core(core)] = product(b, core, rows)
+        g_back(b, i, t).start()
+
+    def x_done(t):
+        for n in range(t * subs // 2, (t + 1) * subs // 2):
+            x_first(3, n).wait_recv()
+            for i in range(3):
+                x_relay(i, n).wait_recv()
 
     def add_state(rows, core):
         for i in range(heads // 2):
@@ -326,15 +341,15 @@
     start(w_second, 1, ways)
     start(w_core, 2, near)
     x_pass(3)
-    for n in range(subs):
-        x_first(3, n).wait_recv()
-        for i in range(3):
-            x_relay(i, n).wait_recv()
+    x_done(0)
     for cp in loads[3:]:
         cp.wait()
-    g_part(3, 0)
     wait(w_core, 3, near + far)
-    g_part(3, 1)
+    g_half(3, 0, 0)
+    g_half(3, 1, 0)
+    x_done(1)
+    g_half(3, 0, 1)
+    g_half(3, 1, 1)
     wait(w_third, 2, ways)
     start(w_core, 2, far)
     g_part(2, 0)
@@ -355,7 +370,8 @@
     for b in (3, 2, 1):
         rows = pl.ds(pl.multiple_of(layer((1, -2, 3)[b - 1]) // 2 * quarter, quarter), quarter)
         for i in range(2):
-            g_back(b, i).wait_recv()
+            g_back(b, i, 0).wait_recv()
+            g_back(b, i, 1).wait_recv()
             add_state(rows, lax.rem(c + i, 2))
     qst_b[...] = qst[...].astype(BF)
     phase1(1, qst_b)
@@ -365,12 +381,6 @@
         if i == AT3:
             phase3(1, suf)
         part()
-    phase4(1, suf)
-    for h in range(heads):
-        sh = suf[col(h), :]
-        kg[:, col(h)] = (factor * (kacc[:, col(h)] + mm(v[:, col(h)], sh, NT))).astype(BF)
-        vg[:, col(h)] = (factor * (vacc[:, col(h)] + mm(k[:, col(h)], sh, NN))).astype(BF)
-
     for n in range(subs):
         for i in range(4):
             x_first(i, n).wait_send()
@@ -386,13 +396,22 @@
         for key in near + far:
             w_core(b, *key).wait_send()
         for i in range(2):
-            g_back(b, i).wait_send()
+            g_back(b, i, 0).wait_send()
+            g_back(b, i, 1).wait_send()
     for which, st, fin in ((0, kst, pre), (1, qst_b, suf)):
         for d in range(1, LANES):
             ex1(which, st, d).wait_send()
-            ex3(which, fin, d).wait_send()
+            if which == 0:
+                ex3(which, fin, d).wait_send()
         for d in range(1, rows_n):
             ex2(which, d).wait_send()
+    phase4(1, suf)
+    for h in range(heads):
+        sh = suf[col(h), :]
+        kg[:, col(h)] = (factor * (kacc[:, col(h)] + mm(v[:, col(h)], sh, NT))).astype(BF)
+        vg[:, col(h)] = (factor * (vacc[:, col(h)] + mm(k[:, col(h)], sh, NN))).astype(BF)
+    for d in range(1, LANES):
+        ex3(1, suf, d).wait_send()
 
 
 def on_device(queries, keys, values, out_grad, out_weight):
@@ -447,8 +466,8 @@
             dma((3, 2, 2)),
             dma((3, 2, rows_n)),
             dma((3, 2, rows_n)),
-            dma((3, 2)),
-            dma((3, 2)),
+            dma((3, 2, 2)),
+            dma((3, 2, 2)),
             dma((2, LANES)),
             dma((2, LANES)),
             dma((2, rows_n)),

time: 98.2 us -> 95.4 us (0.971)
  Pallas kernels: 95.7 us -> 92.9 us
    pallas_call x1, Pallas kernels: 95.7 us -> 92.9 us  [on_device(): pl.pallas_call(functools.partial(kernel, factor, zs, rows_n, heads), out_...]
where the time goes in v5:
time: 95.4 us; the launch traced here: 95.3 us
  Pallas kernels  92.9 us (97%)
  local copies, waits for them, and re-layouts  1.73 us (2%)
    pallas_call x1, Pallas kernels, on_device(): pl.pallas_call(functools.partial(kernel, factor, zs, rows_n, heads), out_...  92.9 us

profile of v5, /device:TPU:1, one launch (start us, length us, event | category | flops | bytes accessed | tf_op | source)
XLA Modules:
  0.0 95.3 jit_solution(6003624619827812847)
XLA Ops:
  0.6 92.9 %shard_map.76 = bf16[3,1024,512]{2,1,0:T(8,128)(2,1)S(1)} custom-call(bf16[1024,512]{1,0:T(8,128)(2,1)} %q_hbm.1, bf16[1024,512]{1,0:T(8,128)(2,1)} %k_hbm.1, bf16[1024,512]{1,0:T(8,128)(2,1)} %v_hbm.1, bf16[1024,512]{1,0:T(8,128)(2,1)} %x_hbm.1, bf16[2,4,4,16,4096]{4,3,2,1,0:T(8,128)(2,1)} %bitcast.7), custom_call_target="tpu_custom_call" | custom-call | flops 10737418240 | bytes 16777216 | tf_op jit(solution)/shard_map/pallas_call | solution.py:429
  93.6 1.7 %slice_bitcast_fusion = (bf16[1024,512]{1,0:T(8,128)(2,1)}, bf16[1024,512]{1,0:T(8,128)(2,1)}, bf16[1024,512]{1,0:T(8,128)(2,1)}) fusion(bf16[3,1024,512]{2,1,0:T(8,128)(2,1)S(1)} %shard_map.76), kind=kLoop, calls=%fused_computation | loop fusion | bytes 6291456 | tf_op jit(solution)/shard_map/squeeze | solution.py:487

commit v6 on v5

--- a/solution.py
+++ b/solution.py
@@ -11,8 +11,8 @@
 HD = 128
 CH = 64
 BLK = 256
-AT2 = 13
-AT3 = 24
+AT2 = 10
+AT3 = 20
 LANES = 8
 BF = jnp.bfloat16
 F32 = jnp.float32
@@ -96,9 +96,8 @@
         return remote(piece, piece, fsend.at[i, n], frecv.at[i, n], {"head": layer(-1)})
 
     def w_z(b):
-        return remote(
-            w_hbm.at[c, y, x], w.at[b, c, y, x], wsend.at[b - 1], wrecv.at[b - 1], {"head": layer((1, -2, 3)[b - 1])}
-        )
+        src, to = (w.at[1, c, y, x], -2) if b == 3 else (w_hbm.at[c, y, x], (1, -2)[b - 1])
+        return remote(src, w.at[b, c, y, x], wsend.at[b - 1], wrecv.at[b - 1], {"head": layer(to)})
 
     half = x_hbm.shape[1] * zs // 2
 
@@ -306,8 +305,8 @@
         parts = [functools.partial(kv_part, s0) for s0 in range(0, tok, BLK)]
         return parts + [functools.partial(q_part, r0) for r0 in range(0, tok, BLK)]
 
-    for b in (3, 2, 1):
-        w_z(b).start()
+    w_z(1).start()
+    w_z(2).start()
     loads[0].wait()
     x_send(0)
     loads[1].wait()
@@ -316,24 +315,25 @@
         kst[col(h), :] = mm(k[:, col(h)], v[:, col(h)], TN).astype(BF)
     phase1(0, kst)
     qst[...] = jnp.zeros_like(qst)
-    for b in (3, 2, 1):
+    for b in (1, 2, 3):
         w_z(b).wait_recv()
+        if b == 1:
+            w_z(3).start()
         start(w_first, b, ring3)
-        x_send(4 - b)
+        x_send(b)
     wait(w_first, 3, ring3)
     start(w_second, 3, ways)
     x_pass(0)
-    phase2(0, kst)
     wait(w_first, 2, ring3)
     wait(w_first, 1, ring3)
     x_pass(1)
-    phase3(0, pre)
+    phase2(0, kst)
     wait(w_second, 3, ways)
     start(w_third, 3, ways)
     start(w_second, 2, ways)
     start(w_core, 3, near)
     x_pass(2)
-    phase4(0, pre)
+    phase3(0, pre)
     wait(w_third, 3, ways)
     start(w_core, 3, far)
     wait(w_second, 2, ways)
@@ -347,6 +347,7 @@
     wait(w_core, 3, near + far)
     g_half(3, 0, 0)
     g_half(3, 1, 0)
+    phase4(0, pre)
     x_done(1)
     g_half(3, 0, 1)
     g_half(3, 1, 1)

time: 95.4 us -> 92.5 us (0.970)
  Pallas kernels: 92.9 us -> 90 us
    pallas_call x1, Pallas kernels: 92.9 us -> 90 us  [on_device(): pl.pallas_call(functools.partial(kernel, factor, zs, rows_n, heads), out_...]
where the time goes in v6:
time: 92.5 us; the launch traced here: 92.4 us
  Pallas kernels  90 us (97%)
  local copies, waits for them, and re-layouts  1.73 us (2%)
    pallas_call x1, Pallas kernels, on_device(): pl.pallas_call(functools.partial(kernel, factor, zs, rows_n, heads), out_...  90 us

profile of v6, /device:TPU:1, one launch (start us, length us, event | category | flops | bytes accessed | tf_op | source)
XLA Modules:
  0.0 92.4 jit_solution(18193784022158746914)
XLA Ops:
  0.6 90.0 %shard_map.76 = bf16[3,1024,512]{2,1,0:T(8,128)(2,1)S(1)} custom-call(bf16[1024,512]{1,0:T(8,128)(2,1)} %q_hbm.1, bf16[1024,512]{1,0:T(8,128)(2,1)} %k_hbm.1, bf16[1024,512]{1,0:T(8,128)(2,1)} %v_hbm.1, bf16[1024,512]{1,0:T(8,128)(2,1)} %x_hbm.1, bf16[2,4,4,16,4096]{4,3,2,1,0:T(8,128)(2,1)} %bitcast.7), custom_call_target="tpu_custom_call" | custom-call | flops 10737418240 | bytes 16777216 | tf_op jit(solution)/shard_map/pallas_call | solution.py:430
  90.7 1.7 %slice_bitcast_fusion = (bf16[1024,512]{1,0:T(8,128)(2,1)}, bf16[1024,512]{1,0:T(8,128)(2,1)}, bf16[1024,512]{1,0:T(8,128)(2,1)}) fusion(bf16[3,1024,512]{2,1,0:T(8,128)(2,1)S(1)} %shard_map.76), kind=kLoop, calls=%fused_computation | loop fusion | bytes 6291456 | tf_op jit(solution)/shard_map/squeeze | solution.py:488
